TPU v7x, 768 devices: a whole 4x8x12 slice. The times are simulated.
768 devices in a mesh: section: 24 (over z, y_hi), dp: 32 (over x, y_lo, core).
Axes of the slice: x: 4, y: 8 (y_hi: 2, y_lo: 4; y = y_hi * 4 + y_lo), z: 12, core: 2. Of those that a mesh axis runs over, the one named last changes fastest.
Arguments:
- feed_down: bfloat16 [24, 2048, 4096], P('section', 'dp'), may hold values from -6 to 6
- feed_up: bfloat16 [24, 2048, 4096], P('section', 'dp'), may hold values from -6 to 6
- cotangent_down: bfloat16 [24, 2048, 4096], P('section', 'dp'), may hold values from -6 to 6
- cotangent_up: bfloat16 [24, 2048, 4096], P('section', 'dp'), may hold values from -6 to 6
- roster: int32 [24, 2, 2], P('section'), may hold values from 0 to 1, each once within a row
- value_weight: bfloat16 [24, 4096, 512], P('section'), may hold values from -0.09375 to 0.09375
Outputs:
- next_down: bfloat16 [24, 2048, 4096], P('section', 'dp')
- next_up: bfloat16 [24, 2048, 4096], P('section', 'dp')
- back_down: bfloat16 [24, 2048, 4096], P('section', 'dp')
- back_up: bfloat16 [24, 2048, 4096], P('section', 'dp')
- grad_weight: float32 [24, 4096, 512], P('section', 'dp')
Inputs may be any that keep to these rules, and one draw needn't show every extreme that they name: roster[s, 0, :] and roster[s, 1, :] are each a permutation of the 2 micro-batches: block j of the cotangents that section index s receives for a leg belongs to micro-batch roster[s, leg, j].
All inputs are finite; a program needn't handle non-finite values.
Results may differ from a plain program's by a relative error of at most 0.005.
Values may be sent and summed in bfloat16 or wider, within the bound.
A program may use at most 64 MiB of HBM per device.

v0:
```python
import jax
import jax.numpy as jnp
from jax import lax
from jax.sharding import PartitionSpec as P

KVH = 4
HD = 128
GROUPS = 8


EPSILON = 1e-05


def passed_along(shard, axis, by):
    count = lax.axis_size(axis)
    return lax.ppermute(shard, axis, [(i, (i + by) % count) for i in range(count)])


def normalize(inputs):
    values = inputs.astype(jnp.float32)
    inverse = lax.rsqrt(jnp.mean(values * values, axis=-1, keepdims=True) + EPSILON)
    return (values * inverse, inverse)


def arrange(received, roster_row):
    blocks = roster_row.shape[0]
    match_table = (roster_row[:, None] == jnp.arange(blocks, dtype=jnp.int32)[None, :]).astype(
        jnp.bfloat16
    )
    shaped = received.reshape(blocks, -1)
    placed = jnp.einsum("jx,jm->mx", shaped, match_table, preferred_element_type=jnp.float32)
    return placed.astype(jnp.bfloat16).reshape(received.shape)


def one_leg(inputs, grads, weight):
    scaled, inverse = normalize(inputs)
    normed = scaled.astype(jnp.bfloat16)
    values = jnp.dot(normed, weight, preferred_element_type=jnp.float32)
    row_total = inputs.shape[0]
    spread = jnp.broadcast_to(
        values.reshape(row_total, KVH, 1, HD), (row_total, KVH, GROUPS, HD)
    ).reshape(row_total, -1)
    advanced = (inputs.astype(jnp.float32) + spread).astype(jnp.bfloat16)
    grouped = (
        jnp.sum(grads.astype(jnp.float32).reshape(row_total, KVH, GROUPS, HD), axis=2)
        .reshape(row_total, -1)
        .astype(jnp.bfloat16)
    )
    back_norm = lax.dot_general(
        grouped, weight, (((1,), (1,)), ((), ())), preferred_element_type=jnp.float32
    )
    through = inverse * (back_norm - scaled * jnp.mean(back_norm * scaled, axis=-1, keepdims=True))
    behind = (grads.astype(jnp.float32) + through).astype(jnp.bfloat16)
    return (advanced, behind, normed, grouped)


def on_device(feed_down, feed_up, cotangent_down, cotangent_up, roster, value_weight):
    inputs_down, raw_up = passed_along((feed_down[0], cotangent_up[0]), "section", 1)
    inputs_up, raw_down = passed_along((feed_up[0], cotangent_down[0]), "section", -1)
    weight = value_weight[0]
    grads_down = arrange(raw_down, roster[0, 0])
    grads_up = arrange(raw_up, roster[0, 1])
    advanced_down, behind_down, normed_down, grouped_down = one_leg(inputs_down, grads_down, weight)
    advanced_up, behind_up, normed_up, grouped_up = one_leg(inputs_up, grads_up, weight)
    normed_all = jnp.concatenate([normed_down, normed_up], axis=0)
    grouped_all = jnp.concatenate([grouped_down, grouped_up], axis=0)
    local_rows = normed_all.shape[0]
    members = lax.axis_size("dp")
    factor = float(local_rows * members) ** (-0.5)
    summed = lax.psum_scatter(
        lax.dot_general(
            normed_all, grouped_all, (((0,), (0,)), ((), ())), preferred_element_type=jnp.float32
        ),
        "dp",
        scatter_dimension=0,
        tiled=True,
    )
    return (
        advanced_down[None],
        advanced_up[None],
        behind_down[None],
        behind_up[None],
        (summed * factor)[None],
    )


def solution(mesh):
    placed = (
        P("section", "dp", None),
        P("section", "dp", None),
        P("section", "dp", None),
        P("section", "dp", None),
        P("section", None, None),
        P("section", None, None),
    )
    return jax.shard_map(
        on_device,
        mesh=mesh,
        in_specs=placed,
        out_specs=(
            P("section", "dp", None),
            P("section", "dp", None),
            P("section", "dp", None),
            P("section", "dp", None),
            P("section", "dp", None),
        ),
        check_vma=False,
    )
```

profile of v0, /device:TPU:64, one launch (start us, length us, event | category | flops | bytes accessed | tf_op | source)
XLA Modules:
  0.0 308.0 jit_solution(8608436523347498420)
XLA Ops:
  7.2 6.8 %collective-permute-start.2 = (bf16[64,4096]{1,0:T(8,128)(2,1)}, bf16[64,4096]{1,0:T(8,128)(2,1)S(1)}, u32[]{:S(2)}, u32[]{:S(2)}) collective-permute-start(bf16[64,4096]{1,0:T(8,128)(2,1)} %bitcast.73), channel_id=1, source_target_pairs={{0,736},{32,0},{64,32},{96,64},{128,96},{160,128},{192,160},{224,1... | collective-permute-start | bytes 1572872 | tf_op jit(solution)/shard_map/ppermute | solution.py:16
  14.0 2.9 collective-permute-start.3
  17.0 8.6 %collective-permute-start = (bf16[64,4096]{1,0:T(8,128)(2,1)}, bf16[64,4096]{1,0:T(8,128)(2,1)S(1)}, u32[]{:S(2)}, u32[]{:S(2)}) collective-permute-start(bf16[64,4096]{1,0:T(8,128)(2,1)} %bitcast.75), channel_id=1, source_target_pairs={{0,32},{32,64},{64,96},{96,128},{128,160},{160,192},{192,224},{224... | collective-permute-start | bytes 1572872 | tf_op jit(solution)/shard_map/ppermute | solution.py:16
  25.6 3.3 %collective-permute-start.1 = (bf16[64,4096]{1,0:T(8,128)(2,1)}, bf16[64,4096]{1,0:T(8,128)(2,1)S(1)}, u32[]{:S(2)}, u32[]{:S(2)}) collective-permute-start(bf16[64,4096]{1,0:T(8,128)(2,1)} %bitcast.76), channel_id=1, source_target_pairs={{0,736},{32,0},{64,32},{96,64},{128,96},{160,128},{192,160},{224,1... | collective-permute-start | bytes 1572872 | tf_op jit(solution)/shard_map/ppermute | solution.py:16
  29.7 54.5 %collective-permute-done.2 = bf16[64,4096]{1,0:T(8,128)(2,1)S(1)} collective-permute-done((bf16[64,4096]{1,0:T(8,128)(2,1)}, bf16[64,4096]{1,0:T(8,128)(2,1)S(1)}, u32[]{:S(2)}, u32[]{:S(2)}) %collective-permute-start.2) | collective-permute-done | bytes 524320 | tf_op jit(solution)/shard_map/ppermute | solution.py:16
  84.6 1.2 convolution_convert_fusion.1
  86.5 2.2 reshape.98
  88.7 2.0 convolution_convert_fusion
  90.7 1.2 convert_element_type.103
  91.9 1.3 reshape.100
  93.1 14.6 %collective-permute-done = bf16[64,4096]{1,0:T(8,128)(2,1)S(1)} collective-permute-done((bf16[64,4096]{1,0:T(8,128)(2,1)}, bf16[64,4096]{1,0:T(8,128)(2,1)S(1)}, u32[]{:S(2)}, u32[]{:S(2)}) %collective-permute-start) | collective-permute-done | bytes 524320 | tf_op jit(solution)/shard_map/ppermute | solution.py:16
  108.6 1.4 reduce.1
  110.0 3.8 %fusion.15 = (f32[64]{0:T(128)S(1)}, f32[64,4096]{1,0:T(8,128)S(1)}) fusion(bf16[64,4096]{1,0:T(8,128)(2,1)S(1)} %collective-permute-done, f32[64]{0:T(128)S(1)} %add_rsqrt_fusion.1, bf16[1,4096,512]{2,1,0:T(8,128)(2,1)} %param.11, bf16[8,8,4,128]{3,2,1,0:T(4,128)(2,1)S(1)} %bitcast.72), kind=kOutput, calls=%fused_computation.23 | convolution fusion | flops 269483968 | bytes 5833216 | tf_op jit(solution)/shard_map/dot_general | solution.py:49
  113.9 1.5 fusion.10
  115.4 1.1 fusion.30
  116.5 1.1 fusion.31
  117.6 4.5 %fusion.24 = f32[4096,512]{1,0:T(8,128)} fusion(bf16[64,4096]{1,0:T(8,128)(2,1)S(1)} %get-tuple-element.6, bf16[64,4096]{1,0:T(8,128)(2,1)S(1)} %get-tuple-element.8, bf16[64,512]{1,0:T(8,128)(2,1)S(1)} %get-tuple-element.15, bf16[64,512]{1,0:T(8,128)(2,1)S(1)} %get-tuple-element.16), kind=kOutput, calls=%fused_computation.32 | convolution fusion | flops 539230208 | bytes 9568256 | tf_op jit(solution)/shard_map/dot_general | solution.py:71
  122.2 6.4 %copy.15 = bf16[512,4096]{1,0:T(8,128)(2,1)} copy(bf16[512,4096]{0,1:T(8,128)(2,1)} %bitcast.64) | data formatting | bytes 8388608 | tf_op jit(solution)/shard_map/reshape.35
  128.6 3.7 %fusion.34 = f32[64,4,128]{2,0,1:T(8,128)S(1)} fusion(bf16[4,128,4096]{2,1,0:T(8,128)(2,1)} %bitcast.65, bf16[64,4096]{1,0:T(8,128)(2,1)S(1)} %get-tuple-element.8), kind=kOutput, calls=%fused_computation.42 | convolution fusion | flops 268435456 | bytes 4849664 | tf_op jit(solution)/shard_map/dot_general | solution.py:38
  132.4 1.4 fusion.32
  134.0 1.4 fusion.28
  135.6 1.4 fusion.29
  137.0 162.5 %reduce-scatter.2.cloned.1.call-done = f32[128,512]{1,0:T(8,128)} async-done(((f32[4096,512]{1,0:T(8,128)}), f32[128,512]{1,0:T(8,128)}) %reduce-scatter.2.cloned.1.call-update) | async-done | bytes 262160 | tf_op jit(solution)/shard_map/reduce_scatter | solution.py:70
  299.5 1.7 multiply_bitcast_fusion
  (26 shorter events, 3.1 us)
Async XLA Ops:
  7.2 292.3 %reduce-scatter.2.cloned.1.call-start = ((), (), s32[]{:S(2)}) async-start(), calls=%async_computation.1 | async-start | bytes 8650752 | tf_op jit(solution)/shard_map/reduce_scatter | solution.py:70
  7.2 77.0 %collective-permute-start.2 = (bf16[64,4096]{1,0:T(8,128)(2,1)}, bf16[64,4096]{1,0:T(8,128)(2,1)S(1)}, u32[]{:S(2)}, u32[]{:S(2)}) collective-permute-start(bf16[64,4096]{1,0:T(8,128)(2,1)} %bitcast.73), channel_id=1, source_target_pairs={{0,736},{32,0},{64,32},{96,64},{128,96},{160,128},{192,160},{224,1... | collective-permute-start | bytes 1572872 | tf_op jit(solution)/shard_map/ppermute | solution.py:16
  14.0 72.4 %collective-permute-start.3 = (bf16[64,4096]{1,0:T(8,128)(2,1)}, bf16[64,4096]{1,0:T(8,128)(2,1)}, u32[]{:S(2)}, u32[]{:S(2)}) collective-permute-start(bf16[64,4096]{1,0:T(8,128)(2,1)} %bitcast.74), channel_id=1, source_target_pairs={{0,32},{32,64},{64,96},{96,128},{128,160},{160,192},{192,224},{224... | collective-permute-start | bytes 1572872 | tf_op jit(solution)/shard_map/ppermute | solution.py:16
  17.0 90.8 %collective-permute-start = (bf16[64,4096]{1,0:T(8,128)(2,1)}, bf16[64,4096]{1,0:T(8,128)(2,1)S(1)}, u32[]{:S(2)}, u32[]{:S(2)}) collective-permute-start(bf16[64,4096]{1,0:T(8,128)(2,1)} %bitcast.75), channel_id=1, source_target_pairs={{0,32},{32,64},{64,96},{96,128},{128,160},{160,192},{192,224},{224... | collective-permute-start | bytes 1572872 | tf_op jit(solution)/shard_map/ppermute | solution.py:16
  25.6 82.4 %collective-permute-start.1 = (bf16[64,4096]{1,0:T(8,128)(2,1)}, bf16[64,4096]{1,0:T(8,128)(2,1)S(1)}, u32[]{:S(2)}, u32[]{:S(2)}) collective-permute-start(bf16[64,4096]{1,0:T(8,128)(2,1)} %bitcast.76), channel_id=1, source_target_pairs={{0,736},{32,0},{64,32},{96,64},{128,96},{160,128},{192,160},{224,1... | collective-permute-start | bytes 1572872 | tf_op jit(solution)/shard_map/ppermute | solution.py:16
  110.0 3.9 %copy-start = (bf16[1,4096,512]{2,1,0:T(8,128)(2,1)S(1)}, bf16[1,4096,512]{2,1,0:T(8,128)(2,1)}, u32[]{:S(2)}) copy-start(bf16[1,4096,512]{2,1,0:T(8,128)(2,1)} %param.11) | copy-start | bytes 12582916
  113.9 2.6 copy-start.2
  128.6 3.8 %copy-start.1 = (bf16[512,4096]{1,0:T(8,128)(2,1)S(1)}, bf16[512,4096]{1,0:T(8,128)(2,1)}, u32[]{:S(2)}) copy-start(bf16[512,4096]{1,0:T(8,128)(2,1)} %copy.15) | copy-start | bytes 12582916
Sparse Core Ops, SparseCore 0:
  122.3 177.1 reduce-scatter.1
where the time goes:
time: 309 us; the launch traced here: 308 us
  waiting for transfers between devices  232 us (75%)
  starting transfers between devices  21.7 us (7%)
  matrix products  18.1 us (6%)
  between operations  14.2 us (5%)
  local copies, waits for them, and re-layouts  13.3 us (4%)
  other arithmetic  8.96 us (3%)
    reduce_scatter x1, waiting for transfers between devices, on_device(): lax.psum_scatter(lax.dot_general(normed_all, grouped_all, (((0,), (0,)),...  163 us
    ppermute x4, waiting for transfers between devices, passed_along(): lax.ppermute(shard, axis, [(i, (i + by) % count) for i in range(count)])  69.2 us
    ppermute x4, starting transfers between devices, passed_along(): lax.ppermute(shard, axis, [(i, (i + by) % count) for i in range(count)])  21.7 us
    another operation x1, local copies, waits for them, and re-layouts  6.41 us
  transfers between devices with their start and end apart: 5, of which 3 were waited for; matrix products, arithmetic and copies ran while one was open for 8% of the time, Pallas kernels for 0%

commit v1 on v0

v1 whole, which is shorter than its diff:
```python
import jax
import jax.numpy as jnp
from jax import lax
from jax.experimental import pallas as pl
from jax.experimental.pallas import tpu as pltpu
from jax.sharding import PartitionSpec as P

MESH = pl.DeviceIdType.MESH
F32 = jnp.float32
BF16 = jnp.bfloat16

KVH = 4
HD = 128
GROUPS = 8
SPAN = GROUPS * HD
D = KVH * SPAN
NX, NY, NC = 4, 4, 2
ROWS = 64
BLOCK = 32
TOK = 2 * ROWS
EPSILON = 1e-05
EARLY = KVH - 1


def kernel(
    factor,
    feed_down,
    feed_up,
    cot_down,
    cot_up,
    roster,
    weight,
    next_down,
    next_up,
    back_down,
    back_up,
    grad,
    x_in,
    g_in,
    early_own,
    early_send,
    early_recv,
    w_buf,
    normed,
    turned,
    inverse,
    grouped,
    values,
    through,
    next_buf,
    back_buf,
    keep,
    core_send,
    core_recv,
    x_send,
    x_recv,
    x_total,
    y_send,
    y_recv,
    grad_buf,
    feed_ss,
    feed_rs,
    cot_ss,
    cot_rs,
    early_ss,
    early_rs,
    core_ss,
    core_rs,
    x_ss,
    x_rs,
    y_ss,
    y_rs,
    local_sem,
    out_sem,
):
    sections = lax.axis_size("section")
    s = lax.axis_index("section")
    d = lax.axis_index("dp")
    x = d // (NY * NC)
    y = (d // NC) % NY
    c = d % NC
    ahead = (lax.rem(s + 1, sections), d)
    behind = (lax.rem(s + sections - 1, sections), d)
    twin = (s, d + 1 - 2 * c)

    def x_peer(j):
        return (s, ((x + j) % NX) * (NY * NC) + y * NC + c)

    def y_peer(j):
        return (s, x * (NY * NC) + ((y + j) % NY) * NC + c)

    partners = [ahead, behind, twin]
    partners += [x_peer(j) for j in range(1, NX)]
    partners += [y_peer(j) for j in range(1, NY)]
    barrier = pltpu.get_barrier_semaphore()
    for partner in partners:
        pl.semaphore_signal(barrier, inc=1, device_id=partner, device_id_type=MESH)
    pl.semaphore_wait(barrier, len(partners))

    def remote(src, dst, ss, rs, to):
        return pltpu.make_async_remote_copy(
            src_ref=src, dst_ref=dst, send_sem=ss, recv_sem=rs, device_id=to, device_id_type=MESH
        )

    feeds, cots, earlies = [], [], []
    for h in range(2):
        rows = slice(h * BLOCK, (h + 1) * BLOCK)
        for leg, (src, to) in enumerate(((feed_down, ahead), (feed_up, behind))):
            feeds.append(
                remote(
                    src.at[0, rows, :],
                    x_in.at[leg * ROWS + h * BLOCK : leg * ROWS + (h + 1) * BLOCK, :],
                    feed_ss.at[h, leg],
                    feed_rs.at[h, leg],
                    to,
                )
            )
    for k in range(KVH):
        cols = slice(k * SPAN, (k + 1) * SPAN)
        for leg, (src, to) in enumerate(((cot_down, behind), (cot_up, ahead))):
            cots.append(
                remote(
                    src.at[0, :, cols],
                    g_in.at[leg * ROWS : (leg + 1) * ROWS, cols],
                    cot_ss.at[k, leg],
                    cot_rs.at[k, leg],
                    to,
                )
            )
    for leg, to in enumerate((behind, ahead)):
        earlies.append(
            remote(early_send.at[leg], early_recv.at[leg], early_ss.at[leg], early_rs.at[leg], to)
        )

    for copy in feeds:
        copy.start()
    early_cols = slice(EARLY * SPAN, (EARLY + 1) * SPAN)
    own = [
        pltpu.make_async_copy(src.at[0, :, early_cols], early_own.at[leg], local_sem.at[leg])
        for leg, src in enumerate((cot_down, cot_up))
    ]
    load_w = pltpu.make_async_copy(weight.at[0], w_buf, local_sem.at[2])
    for copy in own:
        copy.start()
    load_w.start()

    def group_sum(ref_tile):
        total = ref_tile(0).astype(F32)
        for j in range(1, GROUPS):
            total = total + ref_tile(j).astype(F32)
        return total

    for leg in range(2):
        own[leg].wait()
        early_send[leg] = group_sum(lambda j: early_own[leg, :, j * HD : (j + 1) * HD]).astype(BF16)
        earlies[leg].start()

    swap = [roster[0, leg, 0] == 1 for leg in range(2)]

    def normalize(h):
        for leg in range(2):

            @pl.loop(0, BLOCK // 16)
            def _(i):
                at = pl.ds(pl.multiple_of(leg * ROWS + h * BLOCK + i * 16, 16), 16)
                val = x_in[at, :].astype(F32)
                inv = lax.rsqrt(jnp.sum(val * val, axis=-1, keepdims=True) * (1.0 / D) + EPSILON)
                inverse[at, :] = jnp.broadcast_to(inv, (16, HD))
                normed[at, :] = (val * inv).astype(BF16)

    def set_grouped(k, leg, parts):
        first, second = parts
        cols = slice(k * HD, (k + 1) * HD)
        grouped[leg * ROWS : leg * ROWS + BLOCK, cols] = jnp.where(swap[leg], second, first).astype(BF16)
        grouped[leg * ROWS + BLOCK : (leg + 1) * ROWS, cols] = jnp.where(swap[leg], first, second).astype(BF16)

    def group(k):
        for leg in range(2):
            parts = []
            for b in range(2):
                lo = leg * ROWS + b * BLOCK
                parts.append(
                    group_sum(lambda j: g_in[lo : lo + BLOCK, k * SPAN + j * HD : k * SPAN + (j + 1) * HD])
                )
            set_grouped(k, leg, parts)

    def core_copy(k):
        return remote(core_send.at[k], core_recv.at[k], core_ss.at[k], core_rs.at[k], twin)

    def x_copy(k, j):
        return remote(
            x_send.at[k, j - 1], x_recv.at[k, j - 1], x_ss.at[k, j - 1], x_rs.at[k, j - 1], x_peer(j)
        )

    def y_copy(k, j):
        return remote(
            y_send.at[k, j - 1], y_recv.at[k, j - 1], y_ss.at[k, j - 1], y_rs.at[k, j - 1], y_peer(j)
        )

    half = NX * NY * HD
    step = 512

    def term(k):
        cols = slice(k * HD, (k + 1) * HD)

        @pl.loop(0, half // step)
        def _(i):
            at = pl.ds(pl.multiple_of(i * step, step), step)
            core_send[k, at, :] = jnp.dot(
                turned[1 - c, at, :], grouped[:, cols], preferred_element_type=F32
            ).astype(BF16)

        core_copy(k).start()

        @pl.loop(0, half // step)
        def _(i):
            at = pl.ds(pl.multiple_of(i * step, step), step)
            keep[k, at, :] = jnp.dot(turned[c, at, :], grouped[:, cols], preferred_element_type=F32)

    quarter = NY * HD

    def over_core(k):
        core_copy(k).wait_recv()
        for j in (2, 1, 3):
            at = pl.ds(pl.multiple_of(((x + j) % NX) * quarter, quarter), quarter)
            x_send[k, j - 1] = (keep[k, at, :] + core_recv[k, at, :].astype(F32)).astype(BF16)
            x_copy(k, j).start()
        at = pl.ds(pl.multiple_of(x * quarter, quarter), quarter)
        x_total[k] = keep[k, at, :] + core_recv[k, at, :].astype(F32)

    def over_x(k):
        for j in range(1, NX):
            x_copy(k, j).wait_recv()
        x_total[k] = (
            x_total[k] + x_recv[k, 0].astype(F32) + x_recv[k, 1].astype(F32) + x_recv[k, 2].astype(F32)
        )
        for j in range(1, NY):
            at = pl.ds(pl.multiple_of(((y + j) % NY) * HD, HD), HD)
            y_send[k, j - 1] = x_total[k, at, :].astype(BF16)
            y_copy(k, j).start()

    def over_y(k):
        for j in range(1, NY):
            y_copy(k, j).wait_recv()
        at = pl.ds(pl.multiple_of(y * HD, HD), HD)
        total = x_total[k, at, :]
        for j in range(1, NY):
            total = total + y_recv[k, j - 1].astype(F32)
        grad_buf[:, k * HD : (k + 1) * HD] = total * factor

    def send_next(k):
        for copy in cots[2 * k : 2 * k + 2]:
            copy.start()

    def sent(copies):
        for copy in copies:
            copy.wait_send()

    def received(copies):
        for copy in copies:
            copy.wait_recv()

    outs = []

    def write(src, dst, i):
        copy = pltpu.make_async_copy(src, dst, out_sem.at[i])
        copy.start()
        outs.append(copy)

    def finish_back(k):
        for leg in range(2):
            for b in range(2):
                lo = leg * ROWS + b * BLOCK
                other = leg * ROWS + (1 - b) * BLOCK

                @pl.loop(0, BLOCK // 16)
                def _(i):
                    at = pl.ds(pl.multiple_of(lo + i * 16, 16), 16)
                    at_other = pl.ds(pl.multiple_of(other + i * 16, 16), 16)
                    cols = slice(k * SPAN, (k + 1) * SPAN)
                    g = jnp.where(
                        swap[leg], g_in[at_other, cols].astype(F32), g_in[at, cols].astype(F32)
                    )
                    back_buf[at, cols] = (g + through[at, cols]).astype(BF16)

        cols = slice(k * SPAN, (k + 1) * SPAN)
        write(back_buf.at[0:ROWS, cols], back_down.at[0, :, cols], 2 * k)
        write(back_buf.at[ROWS:TOK, cols], back_up.at[0, :, cols], 2 * k + 1)

    sent(feeds[0:2])
    send_next(0)
    received(feeds[0:2])
    normalize(0)
    sent(feeds[2:4])
    send_next(1)
    received(feeds[2:4])
    normalize(1)

    @pl.loop(0, NX * NY * NC)
    def _(i):
        cols = pl.ds(pl.multiple_of(i * HD, HD), HD)
        to = pl.ds(pl.multiple_of((i // NC) * HD, HD), HD)
        turned[i % NC, to, :] = normed[:, cols].T

    received(earlies)
    for leg in range(2):
        set_grouped(
            EARLY, leg, [early_recv[leg, 0:BLOCK, :].astype(F32), early_recv[leg, BLOCK:ROWS, :].astype(F32)]
        )
    term(EARLY)

    load_w.wait()
    values[...] = jnp.zeros_like(values)

    @pl.loop(0, D // 512)
    def _(i):
        at = pl.ds(pl.multiple_of(i * 512, 512), 512)
        values[...] += jnp.dot(normed[:, at], w_buf[at, :], preferred_element_type=F32)

    over_core(EARLY)

    @pl.loop(0, TOK // 16)
    def _(i):
        at = pl.ds(pl.multiple_of(i * 16, 16), 16)
        for k in range(KVH):
            val = values[at, k * HD : (k + 1) * HD]
            for j in range(GROUPS):
                cols = slice((k * GROUPS + j) * HD, (k * GROUPS + j + 1) * HD)
                next_buf[at, cols] = (x_in[at, cols].astype(F32) + val).astype(BF16)

    write(next_buf.at[0:ROWS], next_down.at[0], 8)
    write(next_buf.at[ROWS:TOK], next_up.at[0], 9)

    sent(cots[0:2])
    send_next(2)
    received(cots[0:2])
    group(0)
    term(0)
    over_x(EARLY)
    over_core(0)

    sent(cots[2:4])
    send_next(3)
    received(cots[2:4])
    group(1)
    term(1)
    over_y(EARLY)
    over_x(0)
    over_core(1)

    received(cots[4:6])
    group(2)
    term(2)
    over_y(0)
    over_core(2)
    over_x(1)

    @pl.loop(0, D // 512)
    def _(i):
        at = pl.ds(pl.multiple_of(i * 512, 512), 512)
        through[:, at] = lax.dot_general(
            grouped[...], w_buf[at, :], (((1,), (1,)), ((), ())), preferred_element_type=F32
        )

    @pl.loop(0, TOK // 16)
    def _(i):
        at = pl.ds(pl.multiple_of(i * 16, 16), 16)
        inv = inverse[at, 0:1]
        scaled = x_in[at, :].astype(F32) * inv
        back_norm = through[at, :]
        mean = jnp.sum(back_norm * scaled, axis=-1, keepdims=True) * (1.0 / D)
        through[at, :] = inv * (back_norm - scaled * mean)

    over_x(2)
    for k in range(KVH):
        if k != EARLY:
            finish_back(k)
    over_y(1)
    over_y(2)
    write(grad_buf, grad.at[0], 10)

    received(cots[6:8])
    finish_back(EARLY)

    sent(cots[4:8])
    sent(earlies)
    for k in range(KVH):
        core_copy(k).wait_send()
        for j in range(1, NX):
            x_copy(k, j).wait_send()
        for j in range(1, NY):
            y_copy(k, j).wait_send()
    for copy in outs:
        copy.wait()


def on_device(feed_down, feed_up, cotangent_down, cotangent_up, roster, value_weight):
    factor = float(TOK * lax.axis_size("dp")) ** (-0.5)
    sem = pltpu.SemaphoreType.DMA
    half = NX * NY * HD
    return pl.pallas_call(
        lambda *refs: kernel(factor, *refs),
        out_shape=(
            *(jax.ShapeDtypeStruct((1, ROWS, D), BF16) for _ in range(4)),
            jax.ShapeDtypeStruct((1, D // (NX * NY * NC), KVH * HD), F32),
        ),
        in_specs=[pl.BlockSpec(memory_space=pl.ANY)] * 4
        + [pl.BlockSpec(memory_space=pltpu.SMEM), pl.BlockSpec(memory_space=pl.ANY)],
        out_specs=[pl.BlockSpec(memory_space=pl.ANY)] * 5,
        scratch_shapes=[
            pltpu.VMEM((TOK, D), BF16),
            pltpu.VMEM((TOK, D), BF16),
            pltpu.VMEM((2, ROWS, SPAN), BF16),
            pltpu.VMEM((2, ROWS, HD), BF16),
            pltpu.VMEM((2, ROWS, HD), BF16),
            pltpu.VMEM((D, KVH * HD), BF16),
            pltpu.VMEM((TOK, D), BF16),
            pltpu.VMEM((NC, half, TOK), BF16),
            pltpu.VMEM((TOK, HD), F32),
            pltpu.VMEM((TOK, KVH * HD), BF16),
            pltpu.VMEM((TOK, KVH * HD), F32),
            pltpu.VMEM((TOK, D), F32),
            pltpu.VMEM((TOK, D), BF16),
            pltpu.VMEM((TOK, D), BF16),
            pltpu.VMEM((KVH, half, HD), F32),
            pltpu.VMEM((KVH, half, HD), BF16),
            pltpu.VMEM((KVH, half, HD), BF16),
            pltpu.VMEM((KVH, NX - 1, NY * HD, HD), BF16),
            pltpu.VMEM((KVH, NX - 1, NY * HD, HD), BF16),
            pltpu.VMEM((KVH, NY * HD, HD), F32),
            pltpu.VMEM((KVH, NY - 1, HD, HD), BF16),
            pltpu.VMEM((KVH, NY - 1, HD, HD), BF16),
            pltpu.VMEM((HD, KVH * HD), F32),
            sem((2, 2)),
            sem((2, 2)),
            sem((KVH, 2)),
            sem((KVH, 2)),
            sem((2,)),
            sem((2,)),
            sem((KVH,)),
            sem((KVH,)),
            sem((KVH, NX - 1)),
            sem((KVH, NX - 1)),
            sem((KVH, NY - 1)),
            sem((KVH, NY - 1)),
            sem((3,)),
            sem((11,)),
        ],
        compiler_params=pltpu.CompilerParams(
            collective_id=0, has_side_effects=True, vmem_limit_bytes=56 * 1024 * 1024
        ),
        cost_estimate=pl.CostEstimate(flops=1_700_000_000, bytes_accessed=9_000_000, transcendentals=0),
    )(feed_down, feed_up, cotangent_down, cotangent_up, roster, value_weight)


def solution(mesh):
    placed = P("section", "dp", None)
    whole = P("section", None, None)
    return jax.shard_map(
        on_device,
        mesh=mesh,
        in_specs=(placed, placed, placed, placed, whole, whole),
        out_specs=(placed,) * 5,
        check_vma=False,
    )
```

time: 309 us -> 140 us (0.45)
  the two profiles are of different devices: /device:TPU:64 before, /device:TPU:448 now
where the time goes in v1:
time: 140 us; the launch traced here: 139 us
  Pallas kernels  131 us (94%)
  local copies, waits for them, and re-layouts  8.22 us (6%)
    pallas_call x1, Pallas kernels, on_device(): pl.pallas_call(lambda *refs: kernel(factor, *refs), out_shape=(*(jax.Shap...  131 us
    unnamed x7, local copies, waits for them, and re-layouts  8.22 us

profile of v1, /device:TPU:448, one launch (start us, length us, event | category | flops | bytes accessed | tf_op | source)
XLA Modules:
  0.0 139.4 jit_solution(4867950272949533110)
XLA Ops:
  0.6 130.5 %shard_map.101 = (bf16[1,64,4096]{2,1,0:T(8,128)(2,1)}, bf16[1,64,4096]{2,1,0:T(8,128)(2,1)}, bf16[1,64,4096]{2,1,0:T(8,128)(2,1)}, bf16[1,64,4096]{2,1,0:T(8,128)(2,1)}, f32[1,128,512]{2,1,0:T(8,128)}) custom-call(bf16[1,64,4096]{2,1,0:T(8,128)(2,1)} %refs_0_.1, bf16[1,64,4096]{2,1,0:T(8,128)(2,1)} %refs_1_.1, bf16[1,64,4096]{2,1,0:T(8,128)(2,1)} %refs_2_.1, ...), custom_call_target="tpu_custom_call" | custom-call | flops 1700000000 | bytes 9000000 | tf_op jit(solution)/shard_map/pallas_call | solution.py:401
  131.2 0.0 copy-start
  131.2 1.9 %copy.16 = bf16[1,64,4096]{2,1,0:T(8,128)(2,1)} copy(bf16[1,64,4096]{2,1,0:T(8,128)(2,1)} %get-tuple-element.10) | data formatting | bytes 1048576
  133.1 1.9 %copy.17 = bf16[1,64,4096]{2,1,0:T(8,128)(2,1)} copy(bf16[1,64,4096]{2,1,0:T(8,128)(2,1)} %get-tuple-element.11) | data formatting | bytes 1048576
  134.9 1.9 %copy.18 = bf16[1,64,4096]{2,1,0:T(8,128)(2,1)} copy(bf16[1,64,4096]{2,1,0:T(8,128)(2,1)} %get-tuple-element.12) | data formatting | bytes 1048576
  136.8 1.9 %copy.19 = bf16[1,64,4096]{2,1,0:T(8,128)(2,1)} copy(bf16[1,64,4096]{2,1,0:T(8,128)(2,1)} %get-tuple-element.13) | data formatting | bytes 1048576
  138.7 0.0 copy-done
  138.7 0.7 copy.20
Async XLA Ops:
  131.2 7.5 %copy-start = (f32[1,128,512]{2,1,0:T(8,128)S(1)}, f32[1,128,512]{2,1,0:T(8,128)}, u32[]{:S(2)}) copy-start(f32[1,128,512]{2,1,0:T(8,128)} %get-tuple-element.14) | copy-start | bytes 786436

commit v2 on v1

--- a/solution.py
+++ b/solution.py
@@ -19,7 +19,10 @@
 BLOCK = 32
 TOK = 2 * ROWS
 EPSILON = 1e-05
-EARLY = KVH - 1
+PARTS = 2
+WIDE = D // PARTS
+HEADS = KVH // PARTS
+AHEAD = tuple(range(KVH - HEADS, KVH))
 
 
 def kernel(
@@ -47,8 +50,6 @@
     grouped,
     values,
     through,
-    next_buf,
-    back_buf,
     keep,
     core_send,
     core_recv,
@@ -57,7 +58,6 @@
     x_total,
     y_send,
     y_recv,
-    grad_buf,
     feed_ss,
     feed_rs,
     cot_ss,
@@ -71,7 +71,6 @@
     y_ss,
     y_rs,
     local_sem,
-    out_sem,
 ):
     sections = lax.axis_size("section")
     s = lax.axis_index("section")
@@ -79,6 +78,7 @@
     x = d // (NY * NC)
     y = (d // NC) % NY
     c = d % NC
+    onward, back = (next_down, next_up), (back_down, back_up)
     ahead = (lax.rem(s + 1, sections), d)
     behind = (lax.rem(s + sections - 1, sections), d)
     twin = (s, d + 1 - 2 * c)
@@ -95,6 +95,16 @@
     barrier = pltpu.get_barrier_semaphore()
     for partner in partners:
         pl.semaphore_signal(barrier, inc=1, device_id=partner, device_id_type=MESH)
+    own = [
+        pltpu.make_async_copy(
+            src.at[0, :, AHEAD[0] * SPAN : (AHEAD[-1] + 1) * SPAN], early_own.at[leg], local_sem.at[leg]
+        )
+        for leg, src in enumerate((cot_down, cot_up))
+    ]
+    load_w = pltpu.make_async_copy(weight.at[0], w_buf, local_sem.at[2])
+    for copy in own:
+        copy.start()
+    load_w.start()
     pl.semaphore_wait(barrier, len(partners))
 
     def remote(src, dst, ss, rs, to):
@@ -115,8 +125,8 @@
                     to,
                 )
             )
-    for k in range(KVH):
-        cols = slice(k * SPAN, (k + 1) * SPAN)
+    for k in range(PARTS):
+        cols = slice(k * WIDE, (k + 1) * WIDE)
         for leg, (src, to) in enumerate(((cot_down, behind), (cot_up, ahead))):
             cots.append(
                 remote(
@@ -134,16 +144,6 @@
 
     for copy in feeds:
         copy.start()
-    early_cols = slice(EARLY * SPAN, (EARLY + 1) * SPAN)
-    own = [
-        pltpu.make_async_copy(src.at[0, :, early_cols], early_own.at[leg], local_sem.at[leg])
-        for leg, src in enumerate((cot_down, cot_up))
-    ]
-    load_w = pltpu.make_async_copy(weight.at[0], w_buf, local_sem.at[2])
-    for copy in own:
-        copy.start()
-    load_w.start()
-
     def group_sum(ref_tile):
         total = ref_tile(0).astype(F32)
         for j in range(1, GROUPS):
@@ -152,7 +152,10 @@
 
     for leg in range(2):
         own[leg].wait()
-        early_send[leg] = group_sum(lambda j: early_own[leg, :, j * HD : (j + 1) * HD]).astype(BF16)
+        for k in range(len(AHEAD)):
+            early_send[leg, :, k * HD : (k + 1) * HD] = group_sum(
+                lambda j: early_own[leg, :, k * SPAN + j * HD : k * SPAN + (j + 1) * HD]
+            ).astype(BF16)
         earlies[leg].start()
 
     swap = [roster[0, leg, 0] == 1 for leg in range(2)]
@@ -168,9 +171,8 @@
                 inverse[at, :] = jnp.broadcast_to(inv, (16, HD))
                 normed[at, :] = (val * inv).astype(BF16)
 
-    def set_grouped(k, leg, parts):
-        first, second = parts
-        cols = slice(k * HD, (k + 1) * HD)
+    def set_grouped(leg, heads, first, second):
+        cols = slice(heads[0] * HD, (heads[-1] + 1) * HD)
         grouped[leg * ROWS : leg * ROWS + BLOCK, cols] = jnp.where(swap[leg], second, first).astype(BF16)
         grouped[leg * ROWS + BLOCK : (leg + 1) * ROWS, cols] = jnp.where(swap[leg], first, second).astype(BF16)
 
@@ -182,7 +184,7 @@
                 parts.append(
                     group_sum(lambda j: g_in[lo : lo + BLOCK, k * SPAN + j * HD : k * SPAN + (j + 1) * HD])
                 )
-            set_grouped(k, leg, parts)
+            set_grouped(leg, (k,), *parts)
 
     def core_copy(k):
         return remote(core_send.at[k], core_recv.at[k], core_ss.at[k], core_rs.at[k], twin)
@@ -242,11 +244,10 @@
     def over_y(k):
         for j in range(1, NY):
             y_copy(k, j).wait_recv()
-        at = pl.ds(pl.multiple_of(y * HD, HD), HD)
-        total = x_total[k, at, :]
+        total = x_total[k, pl.ds(pl.multiple_of(y * HD, HD), HD), :]
         for j in range(1, NY):
             total = total + y_recv[k, j - 1].astype(F32)
-        grad_buf[:, k * HD : (k + 1) * HD] = total * factor
+        grad[:, k * HD : (k + 1) * HD] = total * factor
 
     def send_next(k):
         for copy in cots[2 * k : 2 * k + 2]:
@@ -259,13 +260,6 @@
     def received(copies):
         for copy in copies:
             copy.wait_recv()
-
-    outs = []
-
-    def write(src, dst, i):
-        copy = pltpu.make_async_copy(src, dst, out_sem.at[i])
-        copy.start()
-        outs.append(copy)
 
     def finish_back(k):
         for leg in range(2):
@@ -281,19 +275,13 @@
                     g = jnp.where(
                         swap[leg], g_in[at_other, cols].astype(F32), g_in[at, cols].astype(F32)
                     )
-                    back_buf[at, cols] = (g + through[at, cols]).astype(BF16)
-
-        cols = slice(k * SPAN, (k + 1) * SPAN)
-        write(back_buf.at[0:ROWS, cols], back_down.at[0, :, cols], 2 * k)
-        write(back_buf.at[ROWS:TOK, cols], back_up.at[0, :, cols], 2 * k + 1)
-
-    sent(feeds[0:2])
+                    to = pl.ds(pl.multiple_of(b * BLOCK + i * 16, 16), 16)
+                    back[leg][to, cols] = (g + through[at, cols]).astype(BF16)
+
+    sent(feeds)
     send_next(0)
-    received(feeds[0:2])
+    received(feeds)
     normalize(0)
-    sent(feeds[2:4])
-    send_next(1)
-    received(feeds[2:4])
     normalize(1)
 
     @pl.loop(0, NX * NY * NC)
@@ -305,9 +293,12 @@
     received(earlies)
     for leg in range(2):
         set_grouped(
-            EARLY, leg, [early_recv[leg, 0:BLOCK, :].astype(F32), early_recv[leg, BLOCK:ROWS, :].astype(F32)]
-        )
-    term(EARLY)
+            leg, AHEAD, early_recv[leg, 0:BLOCK, :].astype(F32), early_recv[leg, BLOCK:ROWS, :].astype(F32)
+        )
+    for k in AHEAD:
+        term(k)
+    for k in AHEAD:
+        over_core(k)
 
     load_w.wait()
     values[...] = jnp.zeros_like(values)
@@ -317,43 +308,29 @@
         at = pl.ds(pl.multiple_of(i * 512, 512), 512)
         values[...] += jnp.dot(normed[:, at], w_buf[at, :], preferred_element_type=F32)
 
-    over_core(EARLY)
-
-    @pl.loop(0, TOK // 16)
-    def _(i):
-        at = pl.ds(pl.multiple_of(i * 16, 16), 16)
-        for k in range(KVH):
-            val = values[at, k * HD : (k + 1) * HD]
-            for j in range(GROUPS):
-                cols = slice((k * GROUPS + j) * HD, (k * GROUPS + j + 1) * HD)
-                next_buf[at, cols] = (x_in[at, cols].astype(F32) + val).astype(BF16)
-
-    write(next_buf.at[0:ROWS], next_down.at[0], 8)
-    write(next_buf.at[ROWS:TOK], next_up.at[0], 9)
+    for leg in range(2):
+
+        @pl.loop(0, ROWS // 16)
+        def _(i):
+            at = pl.ds(pl.multiple_of(leg * ROWS + i * 16, 16), 16)
+            to = pl.ds(pl.multiple_of(i * 16, 16), 16)
+            for k in range(KVH):
+                val = values[at, k * HD : (k + 1) * HD]
+                for j in range(GROUPS):
+                    cols = slice((k * GROUPS + j) * HD, (k * GROUPS + j + 1) * HD)
+                    onward[leg][to, cols] = (x_in[at, cols].astype(F32) + val).astype(BF16)
+
+    for k in AHEAD:
+        over_x(k)
 
     sent(cots[0:2])
-    send_next(2)
+    send_next(1)
     received(cots[0:2])
-    group(0)
-    term(0)
-    over_x(EARLY)
-    over_core(0)
-
-    sent(cots[2:4])
-    send_next(3)
-    received(cots[2:4])
-    group(1)
-    term(1)
-    over_y(EARLY)
-    over_x(0)
-    over_core(1)
-
-    received(cots[4:6])
-    group(2)
-    term(2)
-    over_y(0)
-    over_core(2)
-    over_x(1)
+    for k in range(HEADS):
+        group(k)
+        term(k)
+    for k in range(HEADS):
+        over_core(k)
 
     @pl.loop(0, D // 512)
     def _(i):
@@ -371,18 +348,18 @@
         mean = jnp.sum(back_norm * scaled, axis=-1, keepdims=True) * (1.0 / D)
         through[at, :] = inv * (back_norm - scaled * mean)
 
-    over_x(2)
-    for k in range(KVH):
-        if k != EARLY:
-            finish_back(k)
-    over_y(1)
-    over_y(2)
-    write(grad_buf, grad.at[0], 10)
-
-    received(cots[6:8])
-    finish_back(EARLY)
-
-    sent(cots[4:8])
+    for k in range(HEADS):
+        over_x(k)
+    for k in range(HEADS):
+        finish_back(k)
+
+    received(cots[2:4])
+    for k in AHEAD:
+        finish_back(k)
+    for k in (*AHEAD, *range(HEADS)):
+        over_y(k)
+
+    sent(cots[2:4])
     sent(earlies)
     for k in range(KVH):
         core_copy(k).wait_send()
@@ -390,7 +367,13 @@
             x_copy(k, j).wait_send()
         for j in range(1, NY):
             y_copy(k, j).wait_send()
-    for copy in outs:
+
+
+def write_out(*refs):
+    copies = [pltpu.make_async_copy(refs[i], refs[5 + i].at[0], refs[10].at[i]) for i in range(5)]
+    for copy in copies:
+        copy.start()
+    for copy in copies:
         copy.wait()
 
 
@@ -398,21 +381,21 @@
     factor = float(TOK * lax.axis_size("dp")) ** (-0.5)
     sem = pltpu.SemaphoreType.DMA
     half = NX * NY * HD
-    return pl.pallas_call(
+    results = pl.pallas_call(
         lambda *refs: kernel(factor, *refs),
         out_shape=(
-            *(jax.ShapeDtypeStruct((1, ROWS, D), BF16) for _ in range(4)),
-            jax.ShapeDtypeStruct((1, D // (NX * NY * NC), KVH * HD), F32),
+            *(pltpu.VMEM((ROWS, D), BF16) for _ in range(4)),
+            pltpu.VMEM((HD, KVH * HD), F32),
         ),
         in_specs=[pl.BlockSpec(memory_space=pl.ANY)] * 4
         + [pl.BlockSpec(memory_space=pltpu.SMEM), pl.BlockSpec(memory_space=pl.ANY)],
-        out_specs=[pl.BlockSpec(memory_space=pl.ANY)] * 5,
+        out_specs=[pl.BlockSpec(memory_space=pltpu.VMEM)] * 5,
         scratch_shapes=[
             pltpu.VMEM((TOK, D), BF16),
             pltpu.VMEM((TOK, D), BF16),
-            pltpu.VMEM((2, ROWS, SPAN), BF16),
-            pltpu.VMEM((2, ROWS, HD), BF16),
-            pltpu.VMEM((2, ROWS, HD), BF16),
+            pltpu.VMEM((2, ROWS, HEADS * SPAN), BF16),
+            pltpu.VMEM((2, ROWS, HEADS * HD), BF16),
+            pltpu.VMEM((2, ROWS, HEADS * HD), BF16),
             pltpu.VMEM((D, KVH * HD), BF16),
             pltpu.VMEM((TOK, D), BF16),
             pltpu.VMEM((NC, half, TOK), BF16),
@@ -420,8 +403,6 @@
             pltpu.VMEM((TOK, KVH * HD), BF16),
             pltpu.VMEM((TOK, KVH * HD), F32),
             pltpu.VMEM((TOK, D), F32),
-            pltpu.VMEM((TOK, D), BF16),
-            pltpu.VMEM((TOK, D), BF16),
             pltpu.VMEM((KVH, half, HD), F32),
             pltpu.VMEM((KVH, half, HD), BF16),
             pltpu.VMEM((KVH, half, HD), BF16),
@@ -430,11 +411,10 @@
             pltpu.VMEM((KVH, NY * HD, HD), F32),
             pltpu.VMEM((KVH, NY - 1, HD, HD), BF16),
             pltpu.VMEM((KVH, NY - 1, HD, HD), BF16),
-            pltpu.VMEM((HD, KVH * HD), F32),
             sem((2, 2)),
             sem((2, 2)),
-            sem((KVH, 2)),
-            sem((KVH, 2)),
+            sem((PARTS, 2)),
+            sem((PARTS, 2)),
             sem((2,)),
             sem((2,)),
             sem((KVH,)),
@@ -444,13 +424,20 @@
             sem((KVH, NY - 1)),
             sem((KVH, NY - 1)),
             sem((3,)),
-            sem((11,)),
         ],
         compiler_params=pltpu.CompilerParams(
             collective_id=0, has_side_effects=True, vmem_limit_bytes=56 * 1024 * 1024
         ),
         cost_estimate=pl.CostEstimate(flops=1_700_000_000, bytes_accessed=9_000_000, transcendentals=0),
     )(feed_down, feed_up, cotangent_down, cotangent_up, roster, value_weight)
+    results = [pltpu.with_memory_space_constraint(one, pltpu.VMEM) for one in results]
+    return pl.pallas_call(
+        write_out,
+        out_shape=tuple(jax.ShapeDtypeStruct((1, *one.shape), one.dtype) for one in results),
+        in_specs=[pl.BlockSpec(memory_space=pltpu.VMEM)] * 5,
+        out_specs=[pl.BlockSpec(memory_space=pl.ANY)] * 5,
+        scratch_shapes=[sem((5,))],
+    )(*results)
 
 
 def solution(mesh):

time: 140 us -> 128 us (0.914)
  the two profiles are of different devices: /device:TPU:448 before, /device:TPU:8 now
where the time goes in v2:
time: 128 us; the launch traced here: 127 us
  Pallas kernels  127 us (99%)
    pallas_call x1, Pallas kernels, on_device(): pl.pallas_call(lambda *refs: kernel(factor, *refs), out_shape=(*(pltpu.VM...  125 us

profile of v2, /device:TPU:8, one launch (start us, length us, event | category | flops | bytes accessed | tf_op | source)
XLA Modules:
  0.0 127.4 jit_solution(3199528185605057264)
XLA Ops:
  0.6 125.3 %shard_map.101 = (bf16[64,4096]{1,0:T(8,128)(2,1)S(1)}, bf16[64,4096]{1,0:T(8,128)(2,1)S(1)}, bf16[64,4096]{1,0:T(8,128)(2,1)S(1)}, bf16[64,4096]{1,0:T(8,128)(2,1)S(1)}, f32[128,512]{1,0:T(8,128)S(1)}) custom-call(bf16[1,64,4096]{2,1,0:T(8,128)(2,1)} %refs_0_.1, bf16[1,64,4096]{2,1,0:T(8,128)(2,1)} %refs_1_.1, bf16[1,64,4096]{2,1,0:T(8,128)(2,1)} %refs_2_.1, ...), custom_call_target="tpu_custom_call" | custom-call | flops 1700000000 | bytes 9000000 | tf_op jit(solution)/shard_map/pallas_call | solution.py:384
  125.9 1.4 %shard_map.102 = (bf16[1,64,4096]{2,1,0:T(8,128)(2,1)}, bf16[1,64,4096]{2,1,0:T(8,128)(2,1)}, bf16[1,64,4096]{2,1,0:T(8,128)(2,1)}, bf16[1,64,4096]{2,1,0:T(8,128)(2,1)}, f32[1,128,512]{2,1,0:T(8,128)}) custom-call(bf16[64,4096]{1,0:T(8,128)(2,1)S(1)} %get-tuple-element.10.refs_0_, bf16[64,4096]{1,0:T(8,128)(2,1)S(1)} %get-tuple-element.11.refs_1_, ...), custom_call_target="tpu_custom_call" | custom-call | tf_op jit(solution)/shard_map/pallas_call | solution.py:434

commit v3 on v2

--- a/solution.py
+++ b/solution.py
@@ -19,10 +19,9 @@
 BLOCK = 32
 TOK = 2 * ROWS
 EPSILON = 1e-05
-PARTS = 2
-WIDE = D // PARTS
-HEADS = KVH // PARTS
-AHEAD = tuple(range(KVH - HEADS, KVH))
+CUTS = (0, SPAN, D)
+PARTS = len(CUTS) - 1
+AHEAD = tuple(range(1, KVH))
 
 
 def kernel(
@@ -71,6 +70,7 @@
     y_ss,
     y_rs,
     local_sem,
+    level_sem,
 ):
     sections = lax.axis_size("section")
     s = lax.axis_index("section")
@@ -126,7 +126,7 @@
                 )
             )
     for k in range(PARTS):
-        cols = slice(k * WIDE, (k + 1) * WIDE)
+        cols = slice(CUTS[k], CUTS[k + 1])
         for leg, (src, to) in enumerate(((cot_down, behind), (cot_up, ahead))):
             cots.append(
                 remote(
@@ -261,6 +261,11 @@
         for copy in copies:
             copy.wait_recv()
 
+    def level(i):
+        for j in range(1, NY):
+            pl.semaphore_signal(level_sem.at[i], inc=1, device_id=y_peer(j), device_id_type=MESH)
+        pl.semaphore_wait(level_sem.at[i], NY - 1)
+
     def finish_back(k):
         for leg in range(2):
             for b in range(2):
@@ -279,6 +284,7 @@
                     back[leg][to, cols] = (g + through[at, cols]).astype(BF16)
 
     sent(feeds)
+    level(0)
     send_next(0)
     received(feeds)
     normalize(0)
@@ -299,6 +305,8 @@
         term(k)
     for k in AHEAD:
         over_core(k)
+    sent(cots[0:2])
+    send_next(1)
 
     load_w.wait()
     values[...] = jnp.zeros_like(values)
@@ -320,17 +328,14 @@
                     cols = slice((k * GROUPS + j) * HD, (k * GROUPS + j + 1) * HD)
                     onward[leg][to, cols] = (x_in[at, cols].astype(F32) + val).astype(BF16)
 
-    for k in AHEAD:
-        over_x(k)
-
-    sent(cots[0:2])
-    send_next(1)
+    over_x(1)
+    over_x(2)
+
     received(cots[0:2])
-    for k in range(HEADS):
-        group(k)
-        term(k)
-    for k in range(HEADS):
-        over_core(k)
+    group(0)
+    term(0)
+    over_x(3)
+    over_core(0)
 
     @pl.loop(0, D // 512)
     def _(i):
@@ -348,15 +353,13 @@
         mean = jnp.sum(back_norm * scaled, axis=-1, keepdims=True) * (1.0 / D)
         through[at, :] = inv * (back_norm - scaled * mean)
 
-    for k in range(HEADS):
-        over_x(k)
-    for k in range(HEADS):
-        finish_back(k)
+    over_x(0)
+    finish_back(0)
 
     received(cots[2:4])
     for k in AHEAD:
         finish_back(k)
-    for k in (*AHEAD, *range(HEADS)):
+    for k in (*AHEAD, 0):
         over_y(k)
 
     sent(cots[2:4])
@@ -393,9 +396,9 @@
         scratch_shapes=[
             pltpu.VMEM((TOK, D), BF16),
             pltpu.VMEM((TOK, D), BF16),
-            pltpu.VMEM((2, ROWS, HEADS * SPAN), BF16),
-            pltpu.VMEM((2, ROWS, HEADS * HD), BF16),
-            pltpu.VMEM((2, ROWS, HEADS * HD), BF16),
+            pltpu.VMEM((2, ROWS, len(AHEAD) * SPAN), BF16),
+            pltpu.VMEM((2, ROWS, len(AHEAD) * HD), BF16),
+            pltpu.VMEM((2, ROWS, len(AHEAD) * HD), BF16),
             pltpu.VMEM((D, KVH * HD), BF16),
             pltpu.VMEM((TOK, D), BF16),
             pltpu.VMEM((NC, half, TOK), BF16),
@@ -424,6 +427,7 @@
             sem((KVH, NY - 1)),
             sem((KVH, NY - 1)),
             sem((3,)),
+            pltpu.SemaphoreType.REGULAR((2,)),
         ],
         compiler_params=pltpu.CompilerParams(
             collective_id=0, has_side_effects=True, vmem_limit_bytes=56 * 1024 * 1024

time: 128 us -> 127 us (level)
  the two profiles are of different devices: /device:TPU:8 before, /device:TPU:645 now
where the time goes in v3:
time: 127 us; the launch traced here: 126 us
  Pallas kernels  126 us (99%)
    pallas_call x1, Pallas kernels, on_device(): pl.pallas_call(lambda *refs: kernel(factor, *refs), out_shape=(*(pltpu.VM...  124 us

profile of v3, /device:TPU:645, one launch (start us, length us, event | category | flops | bytes accessed | tf_op | source)
XLA Modules:
  0.0 126.4 jit_solution(9345823813573234853)
XLA Ops:
  0.6 124.3 %shard_map.101 = (bf16[64,4096]{1,0:T(8,128)(2,1)S(1)}, bf16[64,4096]{1,0:T(8,128)(2,1)S(1)}, bf16[64,4096]{1,0:T(8,128)(2,1)S(1)}, bf16[64,4096]{1,0:T(8,128)(2,1)S(1)}, f32[128,512]{1,0:T(8,128)S(1)}) custom-call(bf16[1,64,4096]{2,1,0:T(8,128)(2,1)} %refs_0_.1, bf16[1,64,4096]{2,1,0:T(8,128)(2,1)} %refs_1_.1, bf16[1,64,4096]{2,1,0:T(8,128)(2,1)} %refs_2_.1, ...), custom_call_target="tpu_custom_call" | custom-call | flops 1700000000 | bytes 9000000 | tf_op jit(solution)/shard_map/pallas_call | solution.py:387
  124.9 1.4 %shard_map.102 = (bf16[1,64,4096]{2,1,0:T(8,128)(2,1)}, bf16[1,64,4096]{2,1,0:T(8,128)(2,1)}, bf16[1,64,4096]{2,1,0:T(8,128)(2,1)}, bf16[1,64,4096]{2,1,0:T(8,128)(2,1)}, f32[1,128,512]{2,1,0:T(8,128)}) custom-call(bf16[64,4096]{1,0:T(8,128)(2,1)S(1)} %get-tuple-element.10.refs_0_, bf16[64,4096]{1,0:T(8,128)(2,1)S(1)} %get-tuple-element.11.refs_1_, ...), custom_call_target="tpu_custom_call" | custom-call | tf_op jit(solution)/shard_map/pallas_call | solution.py:438

commit v4 on v3

--- a/solution.py
+++ b/solution.py
@@ -301,10 +301,12 @@
         set_grouped(
             leg, AHEAD, early_recv[leg, 0:BLOCK, :].astype(F32), early_recv[leg, BLOCK:ROWS, :].astype(F32)
         )
-    for k in AHEAD:
-        term(k)
-    for k in AHEAD:
-        over_core(k)
+    term(1)
+    term(2)
+    over_core(1)
+    term(3)
+    over_core(2)
+    over_core(3)
     sent(cots[0:2])
     send_next(1)
 

time: 127 us -> 127 us (level)
  no operation moved by 1% of the time
where the time goes in v4:
time: 127 us
  Pallas kernels  126 us (99%)
    pallas_call x1, Pallas kernels, on_device(): pl.pallas_call(lambda *refs: kernel(factor, *refs), out_shape=(*(pltpu.VM...  125 us

profile of v4, /device:TPU:645, one launch (start us, length us, event | category | flops | bytes accessed | tf_op | source)
XLA Modules:
  0.0 126.7 jit_solution(15482450735919669322)
XLA Ops:
  0.6 124.6 %shard_map.101 = (bf16[64,4096]{1,0:T(8,128)(2,1)S(1)}, bf16[64,4096]{1,0:T(8,128)(2,1)S(1)}, bf16[64,4096]{1,0:T(8,128)(2,1)S(1)}, bf16[64,4096]{1,0:T(8,128)(2,1)S(1)}, f32[128,512]{1,0:T(8,128)S(1)}) custom-call(bf16[1,64,4096]{2,1,0:T(8,128)(2,1)} %refs_0_.1, bf16[1,64,4096]{2,1,0:T(8,128)(2,1)} %refs_1_.1, bf16[1,64,4096]{2,1,0:T(8,128)(2,1)} %refs_2_.1, ...), custom_call_target="tpu_custom_call" | custom-call | flops 1700000000 | bytes 9000000 | tf_op jit(solution)/shard_map/pallas_call | solution.py:389
  125.2 1.4 %shard_map.102 = (bf16[1,64,4096]{2,1,0:T(8,128)(2,1)}, bf16[1,64,4096]{2,1,0:T(8,128)(2,1)}, bf16[1,64,4096]{2,1,0:T(8,128)(2,1)}, bf16[1,64,4096]{2,1,0:T(8,128)(2,1)}, f32[1,128,512]{2,1,0:T(8,128)}) custom-call(bf16[64,4096]{1,0:T(8,128)(2,1)S(1)} %get-tuple-element.10.refs_0_, bf16[64,4096]{1,0:T(8,128)(2,1)S(1)} %get-tuple-element.11.refs_1_, ...), custom_call_target="tpu_custom_call" | custom-call | tf_op jit(solution)/shard_map/pallas_call | solution.py:440
